TPU v7x, 512 devices: a whole 4x4x16 slice. The times are simulated.
512 devices in a mesh: sample: 32 (over z_lo, y), tok: 16 (over z_hi, x, core).
Axes of the slice: x: 4, y: 4, z: 16 (z_hi: 2, z_lo: 8; z = z_hi * 8 + z_lo), core: 2. Of those that a mesh axis runs over, the one named last changes fastest.
Arguments:
- noisy_tokens: bfloat16 [32, 512, 768], P('sample', 'tok'), may hold values from -6 to 6
- pair_bias: bfloat16 [16, 512, 512], P(None, 'tok', 'sample'), may hold values from -3 to 305
- chain_ids: int32 [512], replicated, may hold values from 0 to 7, never falling along the last dimension, each value on 1 to 128 neighbouring positions
- pad_mask: int32 [512], replicated, may hold values 0 or 1
- step_index: int32 [32], P('sample'), may hold values from 0 to 199
- chain_gain: float32 [16], replicated, may hold values from -3 to 3
- w_query: bfloat16 [768, 768], replicated, may hold values from -0.21875 to 0.21875
- w_key: bfloat16 [768, 768], replicated, may hold values from -0.21875 to 0.21875
- w_value: bfloat16 [768, 768], replicated, may hold values from -0.21875 to 0.21875
- w_output: bfloat16 [768, 768], replicated, may hold values from -0.21875 to 0.21875
Outputs:
- denoised: bfloat16 [32, 512, 768], P('sample', 'tok')
Inputs may be any that keep to these rules, and one draw needn't show every extreme that they name: `chain_ids`: chains are contiguous runs of 1 to 128 tokens, numbered in order.
All inputs are finite; a program needn't handle non-finite values.
Results may differ from a plain program's by a relative error of at most 0.0034.
Values may be sent and summed in bfloat16 or wider, within the bound.
A program may use at most 64 MiB of HBM per device.

v0:
```python
import math

import jax
import jax.numpy as jnp
from jax import lax
from jax.sharding import PartitionSpec as P

STEPS = 200


sigma_data = 16.0
sigma_top = 160.0
sigma_low = 0.0004
rho_exp = 7.0


def layer_norm(values):
    xf = values.astype(jnp.float32)
    center = xf - jnp.mean(xf, axis=-1, keepdims=True)
    spread = jnp.mean(center * center, axis=-1, keepdims=True)
    return (center * lax.rsqrt(spread + 1e-05)).astype(jnp.bfloat16)


def noise_factors(step_index):
    ratio = step_index.astype(jnp.float32) / (STEPS - 1)
    upper = sigma_top ** (1.0 / rho_exp)
    lower = sigma_low ** (1.0 / rho_exp)
    sigma = sigma_data * (upper + ratio * (lower - upper)) ** rho_exp
    skip_scale = sigma_data**2 / (sigma_data**2 + sigma * sigma)
    out_scale = sigma / jnp.sqrt(sigma * sigma + sigma_data**2)
    return (skip_scale, out_scale)


def project(flat, weight):
    return jnp.dot(flat, weight, preferred_element_type=jnp.float32).astype(jnp.bfloat16)


def shards(
    noisy_tokens,
    pair_bias,
    chain_ids,
    pad_mask,
    step_index,
    chain_gain,
    w_query,
    w_key,
    w_value,
    w_output,
):
    samples, rows, width = noisy_tokens.shape
    heads = chain_gain.shape[0]
    head_size = width // heads
    start = lax.axis_index("tok") * rows
    chain_rows = lax.dynamic_slice_in_dim(chain_ids, start, rows)
    normed = layer_norm(noisy_tokens)
    flat = normed.reshape(samples * rows, width)
    queries = project(flat, w_query).reshape(samples, rows, heads, head_size)
    bias_rows = lax.all_gather(pair_bias, "sample", axis=2, tiled=True)
    everyone = lax.all_gather(normed, "tok", axis=1, tiled=True)
    total = everyone.shape[1]
    every_flat = everyone.reshape(samples * total, width)
    key_rows = project(every_flat, w_key).reshape(samples, total, heads, head_size)
    value_rows = project(every_flat, w_value).reshape(samples, total, heads, head_size)
    same_chain = (chain_rows[:, None] == chain_ids[None, :]).astype(jnp.float32)
    masked = (pad_mask.astype(jnp.float32) - 1.0) * 1000000000.0
    scale_root = jnp.sqrt(jnp.float32(head_size))
    group = math.gcd(heads, 4)
    pieces = []
    for first in range(0, heads, group):
        query_part = queries[:, :, first : first + group]
        key_part = key_rows[:, :, first : first + group]
        value_part = value_rows[:, :, first : first + group]
        scores = jnp.einsum(
            "sihd,sjhd->shij", query_part, key_part, preferred_element_type=jnp.float32
        )
        scores = scores / scale_root
        scores = scores + bias_rows[first : first + group].astype(jnp.float32)[None]
        gains = chain_gain[first : first + group]
        scores = (
            scores
            + gains[None, :, None, None] * same_chain[None, None]
            + masked[None, None, None, :]
        )
        top = jnp.max(scores, axis=-1, keepdims=True)
        expo = jnp.exp(scores - top)
        weights = (expo / jnp.sum(expo, axis=-1, keepdims=True)).astype(jnp.bfloat16)
        attended_part = jnp.einsum(
            "shij,sjhd->sihd", weights, value_part, preferred_element_type=jnp.float32
        )
        pieces.append(attended_part.astype(jnp.bfloat16))
    attended = jnp.concatenate(pieces, axis=2).reshape(samples * rows, width)
    projected = jnp.dot(attended, w_output, preferred_element_type=jnp.float32).reshape(
        samples, rows, width
    )
    skip_scale, out_scale = noise_factors(step_index)
    mixed = (
        skip_scale[:, None, None] * noisy_tokens.astype(jnp.float32)
        + out_scale[:, None, None] * projected
    )
    return mixed.astype(jnp.bfloat16)


def solution(mesh):
    in_specs = (
        P("sample", "tok", None),
        P(None, "tok", "sample"),
        P(),
        P(),
        P("sample"),
        P(),
        P(),
        P(),
        P(),
        P(),
    )
    out_specs = P("sample", "tok", None)
    return jax.shard_map(shards, mesh=mesh, in_specs=in_specs, out_specs=out_specs, check_vma=False)
```

profile of v0, /device:TPU:8, one launch (start us, length us, event | category | flops | bytes accessed | tf_op | source)
XLA Modules:
  0.0 214.3 jit_solution(18400831928374968863)
XLA Ops:
  0.0 1.0 convert_reduce_fusion
  1.0 1.0 fusion.39
  2.0 0.9 fusion.40
  3.5 55.3 %all_gather.6 = bf16[1,512,768]{2,1,0:T(8,128)(2,1)S(1)} all-gather(bf16[1,32,768]{2,1,0:T(8,128)(2,1)S(1)} %fusion.40), channel_id=1, replica_groups=mesh['sample'=32,'tok'=16] {'tok'}, dimensions={1}, use_global_device_ids=true | all-gather | bytes 835584 | tf_op jit(solution)/shard_map/all_gather | solution.py:59
  58.8 0.9 copy-done.5
  59.7 0.8 convolution_convert_fusion.1
  60.5 1.2 copy.32
  61.7 123.6 %all_gather.7 = bf16[16,32,512]{1,0,2:T(8,128)(2,1)S(1)} all-gather(bf16[16,32,16]{1,0,2:T(8,128)(2,1)S(1)} %copy.35), channel_id=1, replica_groups=mesh['sample'=32,'tok'=16] {'sample'}, dimensions={2}, use_global_device_ids=true | all-gather | bytes 540672 | tf_op jit(solution)/shard_map/all_gather | solution.py:58
  185.2 0.8 fusion.46
  186.1 0.9 copy.51
  187.0 3.2 %convolution_convert_fusion = bf16[512,768]{1,0:T(8,128)(2,1)} fusion(bf16[768,768]{1,0:T(8,128)(2,1)} %param.17, bf16[1,512,768]{2,1,0:T(8,128)(2,1)} %copy-done.5), kind=kOutput, calls=%fused_computation.4 | convolution fusion | flops 604372992 | bytes 2752512 | tf_op jit(solution)/shard_map/dot_general | solution.py:35
  190.2 1.4 copy.34
  193.7 1.4 compare_convert_fusion
  195.0 2.2 %convolution_convert_fusion.2 = bf16[32,768]{1,0:T(8,128)(2,1)} fusion(bf16[768,768]{1,0:T(8,128)(2,1)} %param.16, bf16[1,32,768]{2,1,0:T(8,128)(2,1)} %copy-done.6), kind=kOutput, calls=%fused_computation.34 | convolution fusion | flops 37773312 | bytes 1277952 | tf_op jit(solution)/shard_map/dot_general | solution.py:35
  197.3 1.6 reshape.229
  198.9 1.6 fusion.47
  200.5 1.1 fusion.19
  202.5 2.1 fusion.30
  204.6 0.9 copy.49
  205.5 1.1 fusion.18
  206.9 1.3 fusion.29
  208.8 1.3 fusion.28
  210.8 1.4 fusion.27
  213.3 1.0 fusion.26
  (40 shorter events, 5.4 us)
Async XLA Ops:
  0.0 59.7 %copy-start = (bf16[768,768]{1,0:T(8,128)(2,1)S(1)}, bf16[768,768]{1,0:T(8,128)(2,1)}, u32[]{:S(2)}) copy-start(bf16[768,768]{1,0:T(8,128)(2,1)} %param.18) | copy-start | bytes 3538948
  2.9 0.6 copy-start.6
  58.8 0.9 copy-start.5
  60.5 1.2 copy-start.9
  190.2 1.4 copy-start.11
  201.6 0.7 copy-start.3
  206.6 1.8 copy-start.1
  206.6 1.8 copy-start.8
  208.6 1.8 copy-start.7
  210.4 1.8 copy-start.10
  210.6 2.7 %copy-start.2 = (bf16[768,768]{1,0:T(8,128)(2,1)S(1)}, bf16[768,768]{1,0:T(8,128)(2,1)}, u32[]{:S(2)}) copy-start(bf16[768,768]{1,0:T(8,128)(2,1)} %param.19) | copy-start | bytes 3538948
  210.6 2.7 %copy-start.4 = (bf16[1,32,768]{2,1,0:T(8,128)(2,1)S(1)}, bf16[1,32,768]{2,1,0:T(8,128)(2,1)}, u32[]{:S(2)}) copy-start(bf16[1,32,768]{2,1,0:T(8,128)(2,1)} %param.10) | copy-start | bytes 147460
where the time goes:
time: 215 us; the launch traced here: 214 us
  blocking collectives  179 us (83%)
  matrix products  15.7 us (7%)
  local copies, waits for them, and re-layouts  13 us (6%)
  other arithmetic  5.78 us (3%)
    all_gather x1, blocking collectives, shards(): bias_rows = lax.all_gather(pair_bias, 'sample', axis=2, tiled=True)  124 us
    all_gather x1, blocking collectives, shards(): everyone = lax.all_gather(normed, 'tok', axis=1, tiled=True)  55.3 us
    dot_general x3, matrix products, project(): jnp.dot(flat, weight, preferred_element_type=jnp.float32)  6.2 us
    dot_general x4, matrix products, shards(): jnp.einsum('shij,sjhd->sihd', weights, value_part, preferred_element_type...  6.01 us
    unnamed x29, local copies, waits for them, and re-layouts  4.77 us

commit v1 on v0

v1 whole, which is shorter than its diff:
```python
import functools
import math

import jax
import jax.numpy as jnp
from jax import lax
from jax.experimental import pallas as pl
from jax.experimental.pallas import tpu as pltpu
from jax.sharding import PartitionSpec as P

STEPS = 200
SIGMA_DATA = 16.0
SIGMA_TOP = 160.0
SIGMA_LOW = 0.0004
RHO = 7

Y, Z_LO = 4, 8
X, CORES = 4, 2

MESH = pl.DeviceIdType.MESH
F32 = jnp.float32
BF16 = jnp.bfloat16
NEAR = (Z_LO - 1) + (Y - 1) + (X - 1) + (CORES - 1)


def dot(a, b):
    return lax.dot_general(a, b, (((1,), (0,)), ((), ())), preferred_element_type=F32)


def dot_t(a, b):
    return lax.dot_general(a, b, (((1,), (1,)), ((), ())), preferred_element_type=F32)


def kernel(
    x_hbm, bias_hbm, chain_hbm, pad_hbm, step_hbm, gain_hbm, wq_hbm, wk_hbm, wv_hbm, wo_hbm,
    out_ref,
    x_raw, bias_raw, chain_v, pad_v, step_s, gain_s, wq, wk, wv, wo,
    xbuf, bbuf, kbuf, vbuf, qexp, wvt, ebuf, chain_col, mask_col,
    lsem, xs, xr, bzs, bzr, bys, byr, ready,
):
    heads, keys_each, rows = bias_hbm.shape
    width = x_hbm.shape[2]
    half = xbuf.shape[0] // 2
    head_size = width // heads
    lanes = heads * rows

    s, t = lax.axis_index("sample"), lax.axis_index("tok")
    y, zl = s % Y, s // Y
    core, cx, zh = t % CORES, (t // CORES) % X, t // (CORES * X)

    def tok_of(h, x, c):
        return h * (X * CORES) + x * CORES + c

    def other_x(k):
        return (cx + k) % X

    far = (s, tok_of(1 - zh, cx, core))
    sibling = (s, tok_of(zh, cx, 1 - core))
    along_x = [(s, tok_of(zh, other_x(k), core)) for k in range(1, X)]
    along_y = [(zl * Y + (y + k) % Y, t) for k in range(1, Y)]
    along_z = [(((zl + k) % Z_LO) * Y + y, t) for k in range(1, Z_LO)]

    barrier = pltpu.get_barrier_semaphore()

    @pl.when(zh == 0)
    def _():
        pl.semaphore_signal(barrier, inc=1, device_id=far, device_id_type=MESH)

    for who in along_x + [sibling] + along_z + along_y:
        pl.semaphore_signal(barrier, inc=1, device_id=who, device_id_type=MESH)

    loads = [
        pltpu.make_async_copy(src, dst, lsem.at[n])
        for n, (src, dst) in enumerate(
            [
                (x_hbm, x_raw), (bias_hbm, bias_raw), (chain_hbm, chain_v), (pad_hbm, pad_v),
                (step_hbm, step_s), (gain_hbm, gain_s), (wq_hbm, wq), (wk_hbm, wk), (wv_hbm, wv), (wo_hbm, wo),
            ]
        )
    ]
    for load in loads:
        load.start()

    loads[0].wait()
    xf = x_raw[0].astype(F32)
    center = xf - jnp.mean(xf, axis=-1, keepdims=True)
    spread = jnp.mean(center * center, axis=-1, keepdims=True)
    xbuf[t] = (center * lax.rsqrt(spread + 1e-05)).astype(BF16)

    loads[1].wait()
    bbuf[zl, y] = jnp.concatenate([bias_raw[h] for h in range(heads)], axis=1)

    pl.semaphore_wait(barrier, NEAR + zh)

    def send_x(block, n, who):
        copy = pltpu.make_async_remote_copy(
            src_ref=xbuf.at[block], dst_ref=xbuf.at[block], send_sem=xs.at[n], recv_sem=xr.at[block],
            device_id=who, device_id_type=MESH,
        )
        copy.start()
        return copy

    def recv_x(block):
        pltpu.make_async_remote_copy(
            src_ref=xbuf.at[block], dst_ref=xbuf.at[block], send_sem=xs.at[0], recv_sem=xr.at[block],
            device_id=sibling, device_id_type=MESH,
        ).wait_recv()

    sent = []

    @pl.when(zh == 1)
    def _():
        send_x(t, 0, far)
        pl.semaphore_signal(ready, inc=1, device_id=far, device_id_type=MESH)

    sent += [send_x(t, 1 + k, along_x[k]) for k in range(X - 1)]
    sent.append(send_x(t, X, sibling))
    for k, who in enumerate(along_z):
        copy = pltpu.make_async_remote_copy(
            src_ref=bbuf.at[zl, y], dst_ref=bbuf.at[zl, y], send_sem=bzs.at[k], recv_sem=bzr.at[zl],
            device_id=who, device_id_type=MESH,
        )
        copy.start()
        sent.append(copy)

    loads[2].wait()
    loads[3].wait()
    tokens = chain_v.shape[0]
    chain_row = chain_v[...].astype(F32).reshape(1, tokens)
    chain_col[...] = jnp.transpose(jnp.broadcast_to(chain_row, (128, tokens)))
    mask_row = (pad_v[...].astype(F32).reshape(1, tokens) - 1.0) * 1000000000.0
    mask_col[...] = jnp.transpose(jnp.broadcast_to(mask_row, (128, tokens)))
    lane = lax.broadcasted_iota(jnp.int32, (rows, lanes), 1)
    query = lax.broadcasted_iota(jnp.int32, (rows, lanes), 0)
    pick = lane % rows == query
    own_chain = chain_col[pl.ds(pl.multiple_of(t * rows, rows), rows), 0:1]
    query_chain = jnp.sum(jnp.where(pick, own_chain, 0.0), axis=0, keepdims=True)
    loads[4].wait()
    loads[5].wait()
    gain = jnp.zeros((1, lanes), F32)
    lane_head = lax.broadcasted_iota(jnp.int32, (1, lanes), 1) // rows
    for h in range(heads):
        gain = jnp.where(lane_head == h, gain_s[h], gain)

    loads[6].wait()
    queries = dot(xbuf[t], wq[...]).astype(BF16)
    group_heads = heads // 2
    group_width = width // 2
    group_lanes = lanes // 2
    row_head = lax.broadcasted_iota(jnp.int32, (group_lanes, group_width), 0) // rows
    col_head = lax.broadcasted_iota(jnp.int32, (group_lanes, group_width), 1) // head_size
    for g in range(2):
        part = queries[:, g * group_width : (g + 1) * group_width]
        tiled = jnp.concatenate([part] * group_heads, axis=0)
        qexp[g] = jnp.where(row_head == col_head, tiled, jnp.zeros_like(tiled))

    loads[7].wait()
    loads[8].wait()
    wvt[...] = jnp.transpose(wv[...])

    def keys_values(n, which):
        block = xbuf[pl.ds(which * half, half)].reshape(half * rows, width)
        kbuf[n] = dot(block, wk[...]).astype(BF16)
        vbuf[n] = dot_t(wvt[...], block).astype(BF16)

    def scores(n, which):
        first = pl.multiple_of(which * (half * rows), half * rows)
        z_half = which * (Z_LO // 2)
        key = kbuf[n]
        found = jnp.concatenate(
            [dot_t(key[:, g * group_width : (g + 1) * group_width], qexp[g]) for g in range(2)], axis=1
        )
        bias = bbuf[pl.ds(z_half, Z_LO // 2)].reshape(half * rows, lanes).astype(F32)
        same = chain_col[pl.ds(first, half * rows), 0:1] == query_chain
        found = found * (1.0 / math.sqrt(head_size)) + bias
        found = found + jnp.where(same, gain, 0.0)
        found = found + mask_col[pl.ds(first, half * rows), 0:1]
        top = jnp.max(found, axis=0, keepdims=True)
        expo = jnp.exp(found - top)
        ebuf[n] = expo
        return top, jnp.sum(expo, axis=0, keepdims=True)

    for k in range(1, X):
        block = tok_of(zh, other_x(k), core)
        recv_x(block)
        sent.append(send_x(block, X + k, sibling))
    for k in range(X):
        recv_x(tok_of(zh, other_x(k), 1 - core))
    keys_values(0, zh)

    for k in range(1, Z_LO):
        there = (zl + k) % Z_LO
        pltpu.make_async_remote_copy(
            src_ref=bbuf.at[zl, y], dst_ref=bbuf.at[there, y], send_sem=bzs.at[0], recv_sem=bzr.at[there],
            device_id=sibling, device_id_type=MESH,
        ).wait_recv()
    for k, who in enumerate(along_y):
        copy = pltpu.make_async_remote_copy(
            src_ref=bbuf.at[:, y], dst_ref=bbuf.at[:, y], send_sem=bys.at[k], recv_sem=byr.at[y],
            device_id=who, device_id_type=MESH,
        )
        copy.start()
        sent.append(copy)

    @pl.when(zh == 0)
    def _():
        pl.semaphore_wait(ready, 1)
        send_x(t, 0, far)

    block = tok_of(1 - zh, cx, core)
    recv_x(block)
    for k in range(X - 1):
        sent.append(send_x(block, 2 * X + k, along_x[k]))
    sent.append(send_x(block, 3 * X - 1, sibling))

    for k in range(1, Y):
        there = (y + k) % Y
        pltpu.make_async_remote_copy(
            src_ref=bbuf.at[:, y], dst_ref=bbuf.at[:, there], send_sem=bys.at[0], recv_sem=byr.at[there],
            device_id=sibling, device_id_type=MESH,
        ).wait_recv()
    top_0, sum_0 = scores(0, zh)

    for k in range(1, X):
        block = tok_of(1 - zh, other_x(k), core)
        recv_x(block)
        sent.append(send_x(block, 3 * X + k - 1, sibling))
    for k in range(X):
        recv_x(tok_of(1 - zh, other_x(k), 1 - core))
    keys_values(1, 1 - zh)
    top_1, sum_1 = scores(1, 1 - zh)

    top = jnp.maximum(top_0, top_1)
    part_0, part_1 = jnp.exp(top_0 - top), jnp.exp(top_1 - top)
    total = sum_0 * part_0 + sum_1 * part_1
    w_0 = (ebuf[0] * (part_0 / total)).astype(BF16)
    w_1 = (ebuf[1] * (part_1 / total)).astype(BF16)

    feature_head = lax.broadcasted_iota(jnp.int32, (group_width, group_lanes), 0) // head_size
    lane_of = lax.broadcasted_iota(jnp.int32, (group_width, group_lanes), 1) // rows
    place = pick[:, :group_lanes].astype(BF16)
    pieces = []
    for g in range(2):
        f = slice(g * group_width, (g + 1) * group_width)
        l = slice(g * group_lanes, (g + 1) * group_lanes)
        got = dot(vbuf[0, f, :], w_0[:, l]) + dot(vbuf[1, f, :], w_1[:, l])
        kept = jnp.where(feature_head == lane_of, got, 0.0).astype(BF16)
        pieces.append(dot_t(place, kept).astype(BF16))
    attended = jnp.concatenate(pieces, axis=1)

    loads[9].wait()
    projected = dot(attended, wo[...])
    ratio = jnp.full((1, width), step_s[0], jnp.int32).astype(F32) / (STEPS - 1)
    upper, lower = SIGMA_TOP ** (1.0 / RHO), SIGMA_LOW ** (1.0 / RHO)
    base = upper + ratio * (lower - upper)
    square = base * base
    sigma = SIGMA_DATA * (square * square * square * base)
    skip_scale = SIGMA_DATA**2 / (SIGMA_DATA**2 + sigma * sigma)
    out_scale = sigma / jnp.sqrt(sigma * sigma + SIGMA_DATA**2)
    out_ref[0] = (skip_scale * x_raw[0].astype(F32) + out_scale * projected).astype(BF16)

    for copy in sent:
        copy.wait_send()
    pltpu.make_async_remote_copy(
        src_ref=xbuf.at[t], dst_ref=xbuf.at[t], send_sem=xs.at[0], recv_sem=xr.at[t],
        device_id=far, device_id_type=MESH,
    ).wait_send()


def shards(noisy, pair_bias, chain_ids, pad_mask, step_index, chain_gain, w_query, w_key, w_value, w_output):
    samples, rows, width = noisy.shape
    heads, _, keys_each = pair_bias.shape
    tokens = chain_ids.shape[0]
    blocks = tokens // rows
    lanes = heads * rows
    half_rows = tokens // 2
    dma = pltpu.SemaphoreType.DMA
    weight = pltpu.VMEM((width, width), BF16)
    return pl.pallas_call(
        kernel,
        out_shape=jax.ShapeDtypeStruct((samples, rows, width), BF16),
        in_specs=[pl.BlockSpec(memory_space=pltpu.HBM)] * 10,
        out_specs=pl.BlockSpec(memory_space=pltpu.VMEM),
        scratch_shapes=[
            pltpu.VMEM((samples, rows, width), BF16),
            pltpu.VMEM((heads, keys_each, rows), BF16),
            pltpu.VMEM((tokens,), jnp.int32),
            pltpu.VMEM((tokens,), jnp.int32),
            pltpu.SMEM((1,), jnp.int32),
            pltpu.SMEM((heads,), F32),
            weight, weight, weight, weight,
            pltpu.VMEM((blocks, rows, width), BF16),
            pltpu.VMEM((Z_LO, Y, keys_each, lanes), BF16),
            pltpu.VMEM((2, half_rows, width), BF16),
            pltpu.VMEM((2, width, half_rows), BF16),
            pltpu.VMEM((2, lanes // 2, width // 2), BF16),
            weight,
            pltpu.VMEM((2, half_rows, lanes), F32),
            pltpu.VMEM((tokens, 128), F32),
            pltpu.VMEM((tokens, 128), F32),
            dma((10,)),
            dma((4 * X,)),
            dma((blocks,)),
            dma((Z_LO,)),
            dma((Z_LO,)),
            dma((Y,)),
            dma((Y,)),
            pltpu.SemaphoreType.REGULAR,
        ],
        compiler_params=pltpu.CompilerParams(
            collective_id=0, has_side_effects=True, vmem_limit_bytes=56 * 1024 * 1024
        ),
    )(
        noisy, jnp.transpose(pair_bias, (0, 2, 1)), chain_ids, pad_mask, step_index, chain_gain,
        w_query, w_key, w_value, w_output,
    )


def solution(mesh):
    in_specs = (
        P("sample", "tok", None),
        P(None, "tok", "sample"),
        P(),
        P(),
        P("sample"),
        P(),
        P(),
        P(),
        P(),
        P(),
    )
    out_specs = P("sample", "tok", None)
    return jax.shard_map(shards, mesh=mesh, in_specs=in_specs, out_specs=out_specs, check_vma=False)
```

time: 215 us -> 37 us (0.17)
  the two profiles are of different devices: /device:TPU:8 before, /device:TPU:1 now
where the time goes in v1:
time: 37 us; the launch traced here: 36.9 us
  Pallas kernels  34.8 us (94%)
  local copies, waits for them, and re-layouts  1.42 us (4%)
  between operations  0.66 us (2%)
    pallas_call x1, Pallas kernels, shards(): pl.pallas_call(kernel, out_shape=jax.ShapeDtypeStruct((samples, rows, wid...  34.8 us
    unnamed x1, local copies, waits for them, and re-layouts  1.42 us

profile of v1, /device:TPU:1, one launch (start us, length us, event | category | flops | bytes accessed | tf_op | source)
XLA Modules:
  0.0 36.9 jit_solution(16711626046643231393)
XLA Ops:
  0.7 34.8 %shard_map.100 = bf16[1,32,768]{2,1,0:T(8,128)(2,1)} custom-call(bf16[1,32,768]{2,1,0:T(8,128)(2,1)} %x_hbm.1, bf16[16,16,32]{2,1,0:T(8,128)(2,1)} %bitcast.1, s32[512]{0:T(512)} %chain_hbm.1, s32[512]{0:T(512)} %pad_hbm.1, s32[1]{0:T(128)S(6)} %copy.12.step_hbm, f32[16]{0:T(128)} %gain_hbm.1, bf16[768,768]{1,0:T(8,128)(2,1)} %wq_hbm.1, ...), custom_call_target="tpu_custom_call" | custom-call | tf_op jit(solution)/shard_map/pallas_call | solution.py:279
  35.5 1.4 %copy.13 = bf16[1,32,768]{2,1,0:T(8,128)(2,1)} copy(bf16[1,32,768]{2,1,0:T(8,128)(2,1)} %shard_map.100) | data formatting | bytes 98304

commit v2 on v1

v2 whole, which is shorter than its diff:
```python
import functools
import math

import jax
import jax.numpy as jnp
from jax import lax
from jax.experimental import pallas as pl
from jax.experimental.pallas import tpu as pltpu
from jax.sharding import PartitionSpec as P

STEPS = 200
SIGMA_DATA = 16.0
SIGMA_TOP = 160.0
SIGMA_LOW = 0.0004
RHO = 7

Y, Z_LO = 4, 8
X, CORES = 4, 2

MESH = pl.DeviceIdType.MESH
F32 = jnp.float32
BF16 = jnp.bfloat16
QUAD = Z_LO // 2


def dot(a, b):
    return lax.dot_general(a, b, (((1,), (0,)), ((), ())), preferred_element_type=F32)


def dot_t(a, b):
    return lax.dot_general(a, b, (((1,), (1,)), ((), ())), preferred_element_type=F32)


def kernel(
    step_s, x_hbm, bias_hbm, chain_hbm, pad_hbm, gain_hbm, wq_hbm, wk_hbm, wv_hbm, wo_hbm,
    out_ref,
    x_raw, bias_raw, chain_v, pad_v, gain_s, wq, wk, wv, wo,
    xbuf, bbuf, kbuf, vbuf, qexp, wvt, ebuf, wbuf, chain_col, mask_col,
    lsem, xs, xr, bzs, bzr, bys, byr, ready_x, ready_core, ready_y, ready_near, ready_cross, ready_far,
):
    heads, keys_each, rows = bias_hbm.shape
    width = x_hbm.shape[2]
    per_half = xbuf.shape[0] // 2
    half = per_half * rows
    quarter = half // CORES
    head_size = width // heads
    lanes = heads * rows

    s, t = lax.axis_index("sample"), lax.axis_index("tok")
    y, zl = s % Y, s // Y
    core, cx, zh = t % CORES, (t // CORES) % X, t // (CORES * X)
    quad, place_z = zl // QUAD, zl % QUAD
    late = quad

    def tok_of(h, x, c):
        return h * (X * CORES) + x * CORES + c

    def block_of(h, x, c):
        return h * per_half + c * X + x

    def other_x(k):
        return (cx + k) % X

    far = (s, tok_of(1 - zh, cx, core))
    sibling = (s, tok_of(zh, cx, 1 - core))
    along_x = [(s, tok_of(zh, other_x(k), core)) for k in range(1, X)]
    along_x_both = [(s, tok_of(zh, other_x(k), c)) for k in range(1, X) for c in (core, 1 - core)]
    along_y = [(zl * Y + (y + k) % Y, t) for k in range(1, Y)]
    in_quad = [((quad * QUAD + (place_z + k) % QUAD) * Y + y, t) for k in range(1, QUAD)]
    opposite_z = (1 - quad) * QUAD + place_z
    opposite = (opposite_z * Y + y, t)

    def signal(semaphore, who):
        pl.semaphore_signal(semaphore, inc=1, device_id=who, device_id_type=MESH)

    barrier = pltpu.get_barrier_semaphore()

    @pl.when(zh == 0)
    def _():
        signal(barrier, far)

    @pl.when(core == CORES - 1)
    def _():
        signal(barrier, sibling)

    for k in range(1, X):

        @pl.when(cx + k < X)
        def _(k=k):
            signal(barrier, along_x[k - 1])

    for k in range(1, Y):

        @pl.when(y + k < Y)
        def _(k=k):
            signal(barrier, along_y[k - 1])

    for k in range(1, QUAD):

        @pl.when(place_z + k < QUAD)
        def _(k=k):
            signal(barrier, in_quad[k - 1])

    @pl.when(late == 0)
    def _():
        signal(barrier, opposite)

    loads = [
        pltpu.make_async_copy(src, dst, lsem.at[n])
        for n, (src, dst) in enumerate(
            [
                (x_hbm, x_raw), (bias_hbm, bias_raw), (chain_hbm, chain_v), (pad_hbm, pad_v),
                (gain_hbm, gain_s), (wq_hbm, wq), (wk_hbm, wk), (wv_hbm, wv), (wo_hbm, wo),
            ]
        )
    ]
    for load in loads:
        load.start()

    own = block_of(zh, cx, core)
    loads[0].wait()
    xf = x_raw[0].astype(F32)
    center = xf - jnp.mean(xf, axis=-1, keepdims=True)
    spread = jnp.mean(center * center, axis=-1, keepdims=True)
    xbuf[own] = (center * lax.rsqrt(spread + 1e-05)).astype(BF16)

    loads[1].wait()
    bbuf[zl, y] = jnp.concatenate([bias_raw[h] for h in range(heads)], axis=1)

    earlier = zh + (CORES - 1 - core) + cx + y + place_z + late

    @pl.when(earlier > 0)
    def _():
        pl.semaphore_wait(barrier, earlier)

    def x_copy(block, n, who):
        return pltpu.make_async_remote_copy(
            src_ref=xbuf.at[block], dst_ref=xbuf.at[block], send_sem=xs.at[n], recv_sem=xr.at[block],
            device_id=who, device_id_type=MESH,
        )

    def send_x(block, n, who):
        copy = x_copy(block, n, who)
        copy.start()
        return copy

    def recv_x(block):
        x_copy(block, 0, sibling).wait_recv()

    def z_copy(n, who, there=None):
        there = zl if there is None else there
        block = bbuf.at[there, y]
        return pltpu.make_async_remote_copy(
            src_ref=block, dst_ref=block, send_sem=bzs.at[n], recv_sem=bzr.at[there],
            device_id=who, device_id_type=MESH,
        )

    def y_copy(n, part, who, there):
        q = (quad + part) % 2
        return pltpu.make_async_remote_copy(
            src_ref=bbuf.at[pl.ds(q * QUAD, QUAD), y], dst_ref=bbuf.at[pl.ds(q * QUAD, QUAD), there],
            send_sem=bys.at[part * Y + n], recv_sem=byr.at[part * Y + there],
            device_id=who, device_id_type=MESH,
        )

    def hand_on_y(part):
        copies = [y_copy(n, part, who, y) for n, who in enumerate(along_y)]
        for copy in copies:
            copy.start()
        return copies

    @pl.when(zh == 1)
    def _():
        signal(ready_far, far)
        x_copy(own, 0, far).start()

    for k in range(1, X):

        @pl.when(cx + k >= X)
        def _(k=k):
            signal(ready_x, along_x[k - 1])
            x_copy(own, k, along_x[k - 1]).start()

    @pl.when(core == 0)
    def _():
        signal(ready_core, sibling)
        x_copy(own, X, sibling).start()

    for k in range(1, Y):

        @pl.when(y + k >= Y)
        def _(k=k):
            signal(ready_y, along_y[k - 1])

    for k in range(1, QUAD):

        @pl.when(place_z + k >= QUAD)
        def _(k=k):
            signal(ready_near, in_quad[k - 1])
            z_copy(k, in_quad[k - 1]).start()

    @pl.when(late == 1)
    def _():
        signal(ready_cross, opposite)
        z_copy(QUAD, opposite).start()

    @pl.when(core == CORES - 1)
    def _():
        pl.semaphore_wait(ready_core, 1)
        x_copy(own, X, sibling).start()

    @pl.when(cx < X - 1)
    def _():
        pl.semaphore_wait(ready_x, X - 1 - cx)

    for k in range(1, X):

        @pl.when(cx + k < X)
        def _(k=k):
            x_copy(own, k, along_x[k - 1]).start()

    loads[2].wait()
    loads[3].wait()
    tokens = chain_v.shape[0]
    chain_row = chain_v[...].astype(F32).reshape(1, tokens)
    chain_col[...] = jnp.transpose(jnp.broadcast_to(chain_row, (128, tokens))).reshape(chain_col.shape)
    mask_row = (pad_v[...].astype(F32).reshape(1, tokens) - 1.0) * 1000000000.0
    mask_col[...] = jnp.transpose(jnp.broadcast_to(mask_row, (128, tokens))).reshape(mask_col.shape)
    lane = lax.broadcasted_iota(jnp.int32, (rows, lanes), 1)
    query = lax.broadcasted_iota(jnp.int32, (rows, lanes), 0)
    pick = lane % rows == query
    own_chain = chain_col[t // CORES, core][:, 0:1]
    query_chain = jnp.sum(jnp.where(pick, own_chain, 0.0), axis=0, keepdims=True)
    loads[4].wait()
    gain = jnp.zeros((1, lanes), F32)
    lane_head = lax.broadcasted_iota(jnp.int32, (1, lanes), 1) // rows
    for h in range(heads):
        gain = jnp.where(lane_head == h, gain_s[h], gain)

    loads[5].wait()
    queries = dot(xbuf[own], wq[...]).astype(BF16)
    group_heads = heads // 2
    group_width = width // 2
    group_lanes = lanes // 2
    row_head = lax.broadcasted_iota(jnp.int32, (group_lanes, group_width), 0) // rows
    col_head = lax.broadcasted_iota(jnp.int32, (group_lanes, group_width), 1) // head_size
    for g in range(2):
        part = queries[:, g * group_width : (g + 1) * group_width]
        tiled = jnp.concatenate([part] * group_heads, axis=0)
        qexp[g] = jnp.where(row_head == col_head, tiled, jnp.zeros_like(tiled))

    loads[6].wait()
    loads[7].wait()
    wvt[...] = jnp.transpose(wv[...])

    def keys_values(at, count, first):
        block = xbuf[pl.ds(first, count // rows)].reshape(count, width)
        kbuf[at : at + count] = dot(block, wk[...]).astype(BF16)
        vbuf[:, at : at + count] = dot_t(wvt[...], block).astype(BF16)

    def scores(at, h, c):
        key = kbuf[at : at + quarter]
        found = jnp.concatenate(
            [dot_t(key[:, g * group_width : (g + 1) * group_width], qexp[g]) for g in range(2)], axis=1
        )
        bias = bbuf[pl.ds(h * QUAD, QUAD), pl.ds(c * (Y // CORES), Y // CORES)].reshape(quarter, lanes).astype(F32)
        key_chain = chain_col[pl.ds(h * X, X), c].reshape(quarter, 128)[:, 0:1]
        key_mask = mask_col[pl.ds(h * X, X), c].reshape(quarter, 128)[:, 0:1]
        found = found * (1.0 / math.sqrt(head_size)) + bias
        found = found + jnp.where(key_chain == query_chain, gain, 0.0)
        found = found + key_mask
        top = jnp.max(found, axis=0, keepdims=True)
        expo = jnp.exp(found - top)
        ebuf[at : at + quarter] = expo
        return top, jnp.sum(expo, axis=0, keepdims=True)

    sent = []
    for k in range(1, X):
        block = block_of(zh, other_x(k), core)
        recv_x(block)
        sent.append(send_x(block, X + k, sibling))

    @pl.when(place_z < QUAD - 1)
    def _():
        pl.semaphore_wait(ready_near, QUAD - 1 - place_z)

    for k in range(1, QUAD):

        @pl.when(place_z + k < QUAD)
        def _(k=k):
            z_copy(k, in_quad[k - 1]).start()

    @pl.when(late == 0)
    def _():
        pl.semaphore_wait(ready_cross, 1)
        z_copy(QUAD, opposite).start()

    z_copy(0, sibling, opposite_z).wait_recv()
    for k in range(1, QUAD):
        copy = z_copy(QUAD + k, in_quad[k - 1], opposite_z)
        copy.start()
        sent.append(copy)

    for k in range(X):
        recv_x(block_of(zh, other_x(k), 1 - core))
    keys_values(0, half, zh * per_half)

    for k in range(1, QUAD):
        z_copy(0, sibling, quad * QUAD + (place_z + k) % QUAD).wait_recv()

    @pl.when(y < Y - 1)
    def _():
        pl.semaphore_wait(ready_y, Y - 1 - y)

    sent += hand_on_y(0)

    far_block = block_of(1 - zh, cx, core)

    def far_copies():
        return [x_copy(far_block, 2 * X + n, who) for n, who in enumerate([sibling] + along_x_both)]

    def cross_step():
        for k in range(1, QUAD):
            z_copy(0, sibling, (1 - quad) * QUAD + (place_z + k) % QUAD).wait_recv()
        hand_on_y(1)

    def far_step():
        @pl.when(zh == 0)
        def _():
            pl.semaphore_wait(ready_far, 1)
            x_copy(own, 0, far).start()

        recv_x(far_block)
        for copy in far_copies():
            copy.start()

    @pl.when(late == 0)
    def _():
        cross_step()
        far_step()

    @pl.when(late == 1)
    def _():
        far_step()
        cross_step()

    for part in range(2):
        for k in range(1, Y):
            y_copy(0, part, sibling, (y + k) % Y).wait_recv()
    found = [scores(0, zh, 0), scores(quarter, zh, 1)]

    recv_x(block_of(1 - zh, cx, 1 - core))
    for k in range(1, X):
        for c in (core, 1 - core):
            recv_x(block_of(1 - zh, other_x(k), c))
    keys_values(half, half, (1 - zh) * per_half)
    found += [scores(half, 1 - zh, 0), scores(half + quarter, 1 - zh, 1)]

    top = functools.reduce(jnp.maximum, [f[0] for f in found])
    shares = [jnp.exp(f[0] - top) for f in found]
    total = sum(f[1] * share for f, share in zip(found, shares))
    for n, share in enumerate(shares):
        r = slice(n * quarter, (n + 1) * quarter)
        wbuf[r] = (ebuf[r] * (share / total)).astype(BF16)

    feature_head = lax.broadcasted_iota(jnp.int32, (group_width, group_lanes), 0) // head_size
    lane_of = lax.broadcasted_iota(jnp.int32, (group_width, group_lanes), 1) // rows
    place = pick[:, :group_lanes].astype(BF16)
    pieces = []
    for g in range(2):
        f = slice(g * group_width, (g + 1) * group_width)
        l = slice(g * group_lanes, (g + 1) * group_lanes)
        kept = jnp.where(feature_head == lane_of, dot(vbuf[f], wbuf[:, l]), 0.0).astype(BF16)
        pieces.append(dot_t(place, kept).astype(BF16))
    attended = jnp.concatenate(pieces, axis=1)

    loads[8].wait()
    projected = dot(attended, wo[...])
    ratio = jnp.full((1, width), step_s[0], jnp.int32).astype(F32) / (STEPS - 1)
    upper, lower = SIGMA_TOP ** (1.0 / RHO), SIGMA_LOW ** (1.0 / RHO)
    base = upper + ratio * (lower - upper)
    square = base * base
    sigma = SIGMA_DATA * (square * square * square * base)
    skip_scale = SIGMA_DATA**2 / (SIGMA_DATA**2 + sigma * sigma)
    out_scale = sigma / jnp.sqrt(sigma * sigma + SIGMA_DATA**2)
    out_ref[0] = (skip_scale * x_raw[0].astype(F32) + out_scale * projected).astype(BF16)

    for copy in sent + far_copies() + [y_copy(n, 1, sibling, y) for n in range(Y - 1)]:
        copy.wait_send()
    for n in range(X + 1):
        x_copy(own, n, far).wait_send()
    for n in range(1, QUAD + 1):
        z_copy(n, sibling).wait_send()


def shards(noisy, pair_bias, chain_ids, pad_mask, step_index, chain_gain, w_query, w_key, w_value, w_output):
    samples, rows, width = noisy.shape
    heads, _, keys_each = pair_bias.shape
    tokens = chain_ids.shape[0]
    blocks = tokens // rows
    lanes = heads * rows
    dma = pltpu.SemaphoreType.DMA
    weight = pltpu.VMEM((width, width), BF16)
    column = pltpu.VMEM((blocks // CORES, CORES, rows, 128), F32)
    large = [
        noisy, jnp.transpose(pair_bias, (0, 2, 1)), chain_ids, pad_mask, chain_gain,
        w_query, w_key, w_value, w_output,
    ]
    return pl.pallas_call(
        kernel,
        out_shape=jax.ShapeDtypeStruct((samples, rows, width), BF16),
        in_specs=[pl.BlockSpec(memory_space=pltpu.SMEM)] + [pl.BlockSpec(memory_space=pltpu.HBM)] * len(large),
        out_specs=pl.BlockSpec(memory_space=pltpu.VMEM),
        scratch_shapes=[
            pltpu.VMEM((samples, rows, width), BF16),
            pltpu.VMEM((heads, keys_each, rows), BF16),
            pltpu.VMEM((tokens,), jnp.int32),
            pltpu.VMEM((tokens,), jnp.int32),
            pltpu.SMEM((heads,), F32),
            weight, weight, weight, weight,
            pltpu.VMEM((blocks, rows, width), BF16),
            pltpu.VMEM((Z_LO, Y, keys_each, lanes), BF16),
            pltpu.VMEM((tokens, width), BF16),
            pltpu.VMEM((width, tokens), BF16),
            pltpu.VMEM((2, lanes // 2, width // 2), BF16),
            weight,
            pltpu.VMEM((tokens, lanes), F32),
            pltpu.VMEM((tokens, lanes), BF16),
            column, column,
            dma((len(large),)),
            dma((4 * X,)),
            dma((blocks,)),
            dma((Z_LO,)),
            dma((Z_LO,)),
            dma((2 * Y,)),
            dma((2 * Y,)),
            *[pltpu.SemaphoreType.REGULAR] * 6,
        ],
        compiler_params=pltpu.CompilerParams(
            collective_id=0, has_side_effects=True, vmem_limit_bytes=32 * 1024 * 1024
        ),
    )(step_index, *[pltpu.with_memory_space_constraint(a, pltpu.HBM) for a in large])


def solution(mesh):
    in_specs = (
        P("sample", "tok", None),
        P(None, "tok", "sample"),
        P(),
        P(),
        P("sample"),
        P(),
        P(),
        P(),
        P(),
        P(),
    )
    out_specs = P("sample", "tok", None)
    return jax.shard_map(shards, mesh=mesh, in_specs=in_specs, out_specs=out_specs, check_vma=False)
```

time: 37 us -> 31.9 us (0.86)
  the two profiles are of different devices: /device:TPU:1 before, /device:TPU:385 now
where the time goes in v2:
time: 31.9 us; the launch traced here: 31.8 us
  Pallas kernels  30.5 us (96%)
  between operations  0.66 us (2%)
  local copies, waits for them, and re-layouts  0.62 us (2%)
    pallas_call x1, Pallas kernels, shards(): pl.pallas_call(kernel, out_shape=jax.ShapeDtypeStruct((samples, rows, wid...  30.5 us

profile of v2, /device:TPU:385, one launch (start us, length us, event | category | flops | bytes accessed | tf_op | source)
XLA Modules:
  0.0 31.8 jit_solution(11899969601786761140)
XLA Ops:
  0.7 30.5 %shard_map.100 = bf16[1,32,768]{2,1,0:T(8,128)(2,1)S(1)} custom-call(s32[1]{0:T(128)S(6)} %copy.12.step_s, bf16[1,32,768]{2,1,0:T(8,128)(2,1)} %x_hbm.1, bf16[16,16,32]{2,1,0:T(8,128)(2,1)} %bitcast.1, s32[512]{0:T(512)} %chain_hbm.1, s32[512]{0:T(512)} %pad_hbm.1, f32[16]{0:T(128)} %gain_hbm.1, bf16[768,768]{1,0:T(8,128)(2,1)} %wq_hbm.1, ...), custom_call_target="tpu_custom_call" | custom-call | tf_op jit(solution)/shard_map/pallas_call | solution.py:409
  31.2 0.6 %copy.13 = bf16[1,32,768]{2,1,0:T(8,128)(2,1)} copy(bf16[1,32,768]{2,1,0:T(8,128)(2,1)S(1)} %shard_map.100) | data formatting | bytes 98304

commit v3 on v2

v3 whole, which is shorter than its diff:
```python
import functools
import math

import jax
import jax.numpy as jnp
from jax import lax
from jax.experimental import pallas as pl
from jax.experimental.pallas import tpu as pltpu
from jax.sharding import PartitionSpec as P

STEPS = 200
SIGMA_DATA = 16.0
SIGMA_TOP = 160.0
SIGMA_LOW = 0.0004
RHO = 7

Y, Z_LO = 4, 8
X, CORES = 4, 2

MESH = pl.DeviceIdType.MESH
F32 = jnp.float32
BF16 = jnp.bfloat16
QUAD = Z_LO // 2


def layer_norm(values):
    xf = values.astype(F32)
    center = xf - jnp.mean(xf, axis=-1, keepdims=True)
    spread = jnp.mean(center * center, axis=-1, keepdims=True)
    return (center * lax.rsqrt(spread + 1e-05)).astype(BF16)


def dot(a, b):
    return lax.dot_general(a, b, (((1,), (0,)), ((), ())), preferred_element_type=F32)


def dot_t(a, b):
    return lax.dot_general(a, b, (((1,), (1,)), ((), ())), preferred_element_type=F32)


def kernel(
    step_s, x_hbm, bias_hbm, chain_hbm, pad_hbm, gain_hbm, wq_hbm, wk_hbm, wv_hbm, wo_hbm,
    out_ref,
    x_raw, far_raw, bias_raw, small, gain_s, weights,
    xbuf, bbuf, vbuf, qexp, wvt, ebuf, wbuf, chain_col, mask_col,
    lsem, xs, xr, bzs, bzr, bys, byr, ready,
):
    heads, keys_each, rows = bias_hbm.shape
    width = x_hbm.shape[2]
    per_half = xbuf.shape[0] // 2
    half = per_half * rows
    quarter = half // CORES
    head_size = width // heads
    lanes = heads * rows

    s, t = lax.axis_index("sample"), lax.axis_index("tok")
    y, zl = s % Y, s // Y
    core, cx, zh = t % CORES, (t // CORES) % X, t // (CORES * X)
    quad, place_z = zl // QUAD, zl % QUAD
    late = (quad + zh * (place_z // 2)) % 2
    ready_x, ready_core, ready_y, ready_near, ready_cross, ready_far = (ready.at[n] for n in range(6))

    def tok_of(h, x, c):
        return h * (X * CORES) + x * CORES + c

    def block_of(h, x, c):
        return h * per_half + c * X + x

    def other_x(k):
        return (cx + k) % X

    far = (s, tok_of(1 - zh, cx, core))
    sibling = (s, tok_of(zh, cx, 1 - core))
    along_x = [(s, tok_of(zh, other_x(k), core)) for k in range(1, X)]
    along_y = [(zl * Y + (y + k) % Y, t) for k in range(1, Y)]
    in_quad = [((quad * QUAD + (place_z + k) % QUAD) * Y + y, t) for k in range(1, QUAD)]
    opposite_z = (1 - quad) * QUAD + place_z
    opposite = (opposite_z * Y + y, t)

    def signal(semaphore, who):
        pl.semaphore_signal(semaphore, inc=1, device_id=who, device_id_type=MESH)

    barrier = pltpu.get_barrier_semaphore()

    @pl.when(zh == 0)
    def _():
        signal(barrier, far)

    @pl.when(core == CORES - 1)
    def _():
        signal(barrier, sibling)

    for k in range(1, X):

        @pl.when(cx + k < X)
        def _(k=k):
            signal(barrier, along_x[k - 1])

    for k in range(1, Y):

        @pl.when(y + k < Y)
        def _(k=k):
            signal(barrier, along_y[k - 1])

    for k in range(1, QUAD):

        @pl.when(place_z + k < QUAD)
        def _(k=k):
            signal(barrier, in_quad[k - 1])

    @pl.when(late == 0)
    def _():
        signal(barrier, opposite)

    loads = [
        (x_hbm, x_raw, 0), (bias_hbm, bias_raw, 1), (chain_hbm, small.at[0], 2), (pad_hbm, small.at[1], 2),
        (gain_hbm, gain_s, 3), (wq_hbm, weights.at[0], 4), (wk_hbm, weights.at[1], 5), (wv_hbm, weights.at[2], 5),
        (wo_hbm, weights.at[3], 6),
    ]
    for src, dst, n in loads:
        pltpu.make_async_copy(src, dst, lsem.at[n]).start()

    def loaded(ref, n):
        pltpu.make_async_copy(ref, ref, lsem.at[n]).wait()

    def remote(ref, send, recv, who):
        return pltpu.make_async_remote_copy(
            src_ref=ref, dst_ref=ref, send_sem=send, recv_sem=recv, device_id=who, device_id_type=MESH
        )

    FAR = X

    def send_x(block, n, who):
        remote(xbuf.at[block], xs, xr.at[n], who).start()

    def recv_x(blocks, n):
        remote(blocks, xs, xr.at[n], sibling).wait_recv()

    def send_z(n, who, there):
        remote(bbuf.at[there, y], bzs, bzr.at[n], who).start()

    def recv_z(blocks, n):
        remote(blocks, bzs, bzr.at[n], sibling).wait_recv()

    def hand_on_y(part):
        q = (quad + part) % 2
        for who in along_y:
            remote(bbuf.at[pl.ds(q * QUAD, QUAD), y], bys, byr, who).start()

    def send_far():
        pltpu.make_async_remote_copy(
            src_ref=x_hbm, dst_ref=far_raw, send_sem=xs, recv_sem=xr.at[FAR], device_id=far, device_id_type=MESH
        ).start()

    earlier = zh + (CORES - 1 - core) + cx + y + place_z + late

    @pl.when(earlier > 0)
    def _():
        pl.semaphore_wait(barrier, earlier)

    @pl.when(zh == 1)
    def _():
        signal(ready_far, far)
        send_far()

    own = block_of(zh, cx, core)
    loaded(x_raw, 0)
    xbuf[own] = layer_norm(x_raw[0])

    loaded(bias_raw, 1)
    bbuf[zl, y] = jnp.concatenate([bias_raw[h] for h in range(heads)], axis=1)

    for k in range(1, X):

        @pl.when(cx + k >= X)
        def _(k=k):
            signal(ready_x, along_x[k - 1])
            send_x(own, X - k, along_x[k - 1])

    @pl.when(core == 0)
    def _():
        signal(ready_core, sibling)
        send_x(own, 0, sibling)

    for k in range(1, Y):

        @pl.when(y + k >= Y)
        def _(k=k):
            signal(ready_y, along_y[k - 1])

    for k in range(1, QUAD):

        @pl.when(place_z + k >= QUAD)
        def _(k=k):
            signal(ready_near, in_quad[k - 1])
            send_z(0, in_quad[k - 1], zl)

    @pl.when(late == 1)
    def _():
        signal(ready_cross, opposite)
        send_z(1, opposite, zl)

    @pl.when(cx < X - 1)
    def _():
        pl.semaphore_wait(ready_x, X - 1 - cx)

    for k in range(1, X):

        @pl.when(cx + k < X)
        def _(k=k):
            send_x(own, X - k, along_x[k - 1])

    @pl.when(place_z < QUAD - 1)
    def _():
        pl.semaphore_wait(ready_near, QUAD - 1 - place_z)

    for k in range(1, QUAD):

        @pl.when(place_z + k < QUAD)
        def _(k=k):
            send_z(0, in_quad[k - 1], zl)

    @pl.when(late == 0)
    def _():
        pl.semaphore_wait(ready_cross, 1)
        send_z(1, opposite, zl)

    @pl.when(core == CORES - 1)
    def _():
        pl.semaphore_wait(ready_core, 1)
        send_x(own, 0, sibling)

    loaded(small, 2)
    tokens = small.shape[1]
    chain_row = small[0:1].astype(F32)
    chain_col[...] = jnp.transpose(jnp.broadcast_to(chain_row, (128, tokens))).reshape(chain_col.shape)
    mask_row = (small[1:2].astype(F32) - 1.0) * 1000000000.0
    mask_col[...] = jnp.transpose(jnp.broadcast_to(mask_row, (128, tokens))).reshape(mask_col.shape)
    lane = lax.broadcasted_iota(jnp.int32, (rows, lanes), 1)
    query = lax.broadcasted_iota(jnp.int32, (rows, lanes), 0)
    pick = lane % rows == query
    own_chain = chain_col[t // CORES, core][:, 0:1]
    query_chain = jnp.sum(jnp.where(pick, own_chain, 0.0), axis=0, keepdims=True)
    loaded(gain_s, 3)
    gain = jnp.zeros((1, lanes), F32)
    lane_head = lax.broadcasted_iota(jnp.int32, (1, lanes), 1) // rows
    for h in range(heads):
        gain = jnp.where(lane_head == h, gain_s[h], gain)

    loaded(weights.at[0], 4)
    queries = dot(xbuf[own], weights[0]).astype(BF16)
    group_heads = heads // 2
    group_width = width // 2
    group_lanes = lanes // 2
    row_head = lax.broadcasted_iota(jnp.int32, (group_lanes, group_width), 0) // rows
    col_head = lax.broadcasted_iota(jnp.int32, (group_lanes, group_width), 1) // head_size
    for g in range(2):
        part = queries[:, g * group_width : (g + 1) * group_width]
        tiled = jnp.concatenate([part] * group_heads, axis=0)
        qexp[g] = jnp.where(row_head == col_head, tiled, jnp.zeros_like(tiled))

    loaded(weights.at[pl.ds(1, 2)], 5)
    wvt[...] = jnp.transpose(weights[2])

    def values(h):
        block = xbuf[pl.ds(h * per_half, per_half)].reshape(half, width)
        return dot_t(wvt[...], block).astype(BF16)

    def raw_scores(h, c):
        block = xbuf[pl.ds(block_of(h, 0, c), X)].reshape(quarter, width)
        key = dot(block, weights[1]).astype(BF16)
        return jnp.concatenate(
            [dot_t(key[:, g * group_width : (g + 1) * group_width], qexp[g]) for g in range(2)], axis=1
        )

    def scores(found, at, h, c):
        bias = bbuf[pl.ds(h * QUAD, QUAD), pl.ds(c * (Y // CORES), Y // CORES)].reshape(quarter, lanes).astype(F32)
        key_chain = chain_col[pl.ds(h * X, X), c].reshape(quarter, 128)[:, 0:1]
        key_mask = mask_col[pl.ds(h * X, X), c].reshape(quarter, 128)[:, 0:1]
        found = found * (1.0 / math.sqrt(head_size)) + bias
        found = found + jnp.where(key_chain == query_chain, gain, 0.0)
        found = found + key_mask
        top = jnp.max(found, axis=0, keepdims=True)
        expo = jnp.exp(found - top)
        ebuf[at] = expo
        return at, top, jnp.sum(expo, axis=0, keepdims=True)

    def part_of(c):
        return pl.ds(pl.multiple_of(half + c * quarter, quarter), quarter)

    for k in range(1, X):
        block = block_of(zh, other_x(k), core)
        recv_x(xbuf.at[block], k)
        send_x(block, 0, sibling)

    recv_z(bbuf.at[opposite_z, y], 1)
    for who in in_quad:
        send_z(2, who, opposite_z)

    recv_z(bbuf.at[pl.ds(0, QUAD - 1), y], 0)

    @pl.when(y < Y - 1)
    def _():
        pl.semaphore_wait(ready_y, Y - 1 - y)

    hand_on_y(0)

    @pl.when(zh == 0)
    def _():
        pl.semaphore_wait(ready_far, 1)
        send_far()

    recv_x(xbuf.at[pl.ds(0, X)], 0)
    vbuf[:, 0:half] = values(zh)
    for c in range(CORES):
        ebuf[c * quarter : (c + 1) * quarter] = raw_scores(zh, c)

    far_block = block_of(1 - zh, cx, core)

    def cross_step():
        recv_z(bbuf.at[pl.ds(0, QUAD - 1), y], 2)
        hand_on_y(1)

    def far_step():
        recv_x(far_raw, FAR)
        xbuf[far_block] = layer_norm(far_raw[0])
        for k in (2, 1, 3):
            send_x(far_block, FAR + X - k, along_x[k - 1])
        send_x(far_block, 2 * X, sibling)

    @pl.when(late == 0)
    def _():
        cross_step()
        far_step()

    @pl.when(late == 1)
    def _():
        far_step()
        cross_step()

    for k in (1, 3, 2):
        block = block_of(1 - zh, other_x(k), core)
        recv_x(xbuf.at[block], FAR + k)
        send_x(block, 2 * X, sibling)

    remote(bbuf.at[pl.ds(0, 2 * (Y - 1))], bys, byr, sibling).wait_recv()
    found = []
    for c in range(CORES):
        at = pl.ds(c * quarter, quarter)
        found.append(scores(ebuf[at], at, zh, c))
    found.append(scores(raw_scores(1 - zh, core), part_of(core), 1 - zh, core))
    recv_x(xbuf.at[pl.ds(0, X)], 2 * X)
    found.append(scores(raw_scores(1 - zh, 1 - core), part_of(1 - core), 1 - zh, 1 - core))
    vbuf[:, half:] = values(1 - zh)

    top = functools.reduce(jnp.maximum, [f[1] for f in found])
    shares = [jnp.exp(f[1] - top) for f in found]
    total = sum(f[2] * share for f, share in zip(found, shares))
    for (at, _, _), share in zip(found, shares):
        wbuf[at] = (ebuf[at] * (share / total)).astype(BF16)

    feature_head = lax.broadcasted_iota(jnp.int32, (group_width, group_lanes), 0) // head_size
    lane_of = lax.broadcasted_iota(jnp.int32, (group_width, group_lanes), 1) // rows
    place = pick[:, :group_lanes].astype(BF16)
    pieces = []
    for g in range(2):
        f = slice(g * group_width, (g + 1) * group_width)
        l = slice(g * group_lanes, (g + 1) * group_lanes)
        kept = jnp.where(feature_head == lane_of, dot(vbuf[f], wbuf[:, l]), 0.0).astype(BF16)
        pieces.append(dot_t(place, kept).astype(BF16))
    attended = jnp.concatenate(pieces, axis=1)

    loaded(weights.at[3], 6)
    projected = dot(attended, weights[3])
    ratio = jnp.full((1, width), step_s[0], jnp.int32).astype(F32) / (STEPS - 1)
    upper, lower = SIGMA_TOP ** (1.0 / RHO), SIGMA_LOW ** (1.0 / RHO)
    base = upper + ratio * (lower - upper)
    square = base * base
    sigma = SIGMA_DATA * (square * square * square * base)
    skip_scale = SIGMA_DATA**2 / (SIGMA_DATA**2 + sigma * sigma)
    out_scale = sigma / jnp.sqrt(sigma * sigma + SIGMA_DATA**2)
    out_ref[0] = (skip_scale * x_raw[0].astype(F32) + out_scale * projected).astype(BF16)

    remote(xbuf.at[pl.ds(0, 4 * X - 1)], xs, xr.at[0], sibling).wait_send()
    remote(bbuf.at[pl.ds(0, 2 * QUAD - 1), y], bzs, bzr.at[0], sibling).wait_send()
    remote(bbuf.at[pl.ds(0, 2 * (Y - 1))], bys, byr, sibling).wait_send()


def shards(noisy, pair_bias, chain_ids, pad_mask, step_index, chain_gain, w_query, w_key, w_value, w_output):
    samples, rows, width = noisy.shape
    heads, _, keys_each = pair_bias.shape
    tokens = chain_ids.shape[0]
    blocks = tokens // rows
    lanes = heads * rows
    dma = pltpu.SemaphoreType.DMA
    column = pltpu.VMEM((blocks // CORES, CORES, rows, 128), F32)
    large = [
        noisy, jnp.transpose(pair_bias, (0, 2, 1)), chain_ids, pad_mask, chain_gain,
        w_query, w_key, w_value, w_output,
    ]
    return pl.pallas_call(
        kernel,
        out_shape=jax.ShapeDtypeStruct((samples, rows, width), BF16),
        in_specs=[pl.BlockSpec(memory_space=pltpu.SMEM)] + [pl.BlockSpec(memory_space=pltpu.HBM)] * len(large),
        out_specs=pl.BlockSpec(memory_space=pltpu.VMEM),
        scratch_shapes=[
            pltpu.VMEM((samples, rows, width), BF16),
            pltpu.VMEM((samples, rows, width), BF16),
            pltpu.VMEM((heads, keys_each, rows), BF16),
            pltpu.VMEM((2, tokens), jnp.int32),
            pltpu.SMEM((heads,), F32),
            pltpu.VMEM((4, width, width), BF16),
            pltpu.VMEM((blocks, rows, width), BF16),
            pltpu.VMEM((Z_LO, Y, keys_each, lanes), BF16),
            pltpu.VMEM((width, tokens), BF16),
            pltpu.VMEM((2, lanes // 2, width // 2), BF16),
            pltpu.VMEM((width, width), BF16),
            pltpu.VMEM((tokens, lanes), F32),
            pltpu.VMEM((tokens, lanes), BF16),
            column, column,
            dma((7,)),
            dma,
            dma((2 * X + 1,)),
            dma,
            dma((3,)),
            dma,
            dma,
            pltpu.SemaphoreType.REGULAR((6,)),
        ],
        compiler_params=pltpu.CompilerParams(
            collective_id=0, has_side_effects=True, vmem_limit_bytes=32 * 1024 * 1024
        ),
    )(step_index, *[pltpu.with_memory_space_constraint(a, pltpu.HBM) for a in large])


def solution(mesh):
    in_specs = (
        P("sample", "tok", None),
        P(None, "tok", "sample"),
        P(),
        P(),
        P("sample"),
        P(),
        P(),
        P(),
        P(),
        P(),
    )
    out_specs = P("sample", "tok", None)
    return jax.shard_map(shards, mesh=mesh, in_specs=in_specs, out_specs=out_specs, check_vma=False)
```

time: 31.9 us -> 30.5 us (0.956)
  the two profiles are of different devices: /device:TPU:385 before, /device:TPU:457 now
where the time goes in v3:
time: 30.5 us; the launch traced here: 30.4 us
  Pallas kernels  29.1 us (95%)
  between operations  0.66 us (2%)
  local copies, waits for them, and re-layouts  0.62 us (2%)
    pallas_call x1, Pallas kernels, shards(): pl.pallas_call(kernel, out_shape=jax.ShapeDtypeStruct((samples, rows, wid...  29.1 us
    unnamed x1, local copies, waits for them, and re-layouts  0.62 us

profile of v3, /device:TPU:457, one launch (start us, length us, event | category | flops | bytes accessed | tf_op | source)
XLA Modules:
  0.0 30.4 jit_solution(4087749241248552665)
XLA Ops:
  0.7 29.1 %shard_map.100 = bf16[1,32,768]{2,1,0:T(8,128)(2,1)S(1)} custom-call(s32[1]{0:T(128)S(6)} %copy.12.step_s, bf16[1,32,768]{2,1,0:T(8,128)(2,1)} %x_hbm.1, bf16[16,16,32]{2,1,0:T(8,128)(2,1)} %bitcast.1, s32[512]{0:T(512)} %chain_hbm.1, s32[512]{0:T(512)} %pad_hbm.1, f32[16]{0:T(128)} %gain_hbm.1, bf16[768,768]{1,0:T(8,128)(2,1)} %wq_hbm.1, ...), custom_call_target="tpu_custom_call" | custom-call | tf_op jit(solution)/shard_map/pallas_call | solution.py:401
  29.8 0.6 %copy.13 = bf16[1,32,768]{2,1,0:T(8,128)(2,1)} copy(bf16[1,32,768]{2,1,0:T(8,128)(2,1)S(1)} %shard_map.100) | data formatting | bytes 98304

commit v4 on v3

--- a/solution.py
+++ b/solution.py
@@ -42,7 +42,7 @@
     step_s, x_hbm, bias_hbm, chain_hbm, pad_hbm, gain_hbm, wq_hbm, wk_hbm, wv_hbm, wo_hbm,
     out_ref,
     x_raw, far_raw, bias_raw, small, gain_s, weights,
-    xbuf, bbuf, vbuf, qexp, wvt, ebuf, wbuf, chain_col, mask_col,
+    xbuf, bbuf, vbuf, qexp, ebuf, wbuf, chain_col, mask_col,
     lsem, xs, xr, bzs, bzr, bys, byr, ready,
 ):
     heads, keys_each, rows = bias_hbm.shape
@@ -130,8 +130,8 @@
 
     FAR = X
 
-    def send_x(block, n, who):
-        remote(xbuf.at[block], xs, xr.at[n], who).start()
+    def send_x(block, n, who, piece=slice(None)):
+        remote(xbuf.at[block, piece], xs, xr.at[n], who).start()
 
     def recv_x(blocks, n):
         remote(blocks, xs, xr.at[n], sibling).wait_recv()
@@ -142,21 +142,27 @@
     def recv_z(blocks, n):
         remote(blocks, bzs, bzr.at[n], sibling).wait_recv()
 
-    def hand_on_y(part):
-        q = (quad + part) % 2
+    def hand_on_y(blocks):
         for who in along_y:
-            remote(bbuf.at[pl.ds(q * QUAD, QUAD), y], bys, byr, who).start()
+            remote(blocks, bys, byr, who).start()
+
+    PIECES = 2
+    pieces = [pl.ds(p * (rows // PIECES), rows // PIECES) for p in range(PIECES)]
 
     def send_far():
-        pltpu.make_async_remote_copy(
-            src_ref=x_hbm, dst_ref=far_raw, send_sem=xs, recv_sem=xr.at[FAR], device_id=far, device_id_type=MESH
-        ).start()
+        for p, piece in enumerate(pieces):
+            pltpu.make_async_remote_copy(
+                src_ref=x_raw.at[0, piece], dst_ref=far_raw.at[0, piece], send_sem=xs, recv_sem=xr.at[FAR + X * p],
+                device_id=far, device_id_type=MESH,
+            ).start()
 
     earlier = zh + (CORES - 1 - core) + cx + y + place_z + late
 
     @pl.when(earlier > 0)
     def _():
         pl.semaphore_wait(barrier, earlier)
+
+    loaded(x_raw, 0)
 
     @pl.when(zh == 1)
     def _():
@@ -164,12 +170,31 @@
         send_far()
 
     own = block_of(zh, cx, core)
-    loaded(x_raw, 0)
-    xbuf[own] = layer_norm(x_raw[0])
 
     loaded(bias_raw, 1)
     bbuf[zl, y] = jnp.concatenate([bias_raw[h] for h in range(heads)], axis=1)
 
+    for k in range(1, Y):
+
+        @pl.when(y + k >= Y)
+        def _(k=k):
+            signal(ready_y, along_y[k - 1])
+
+    for k in range(1, QUAD):
+
+        @pl.when(place_z + k >= QUAD)
+        def _(k=k):
+            signal(ready_near, in_quad[k - 1])
+            send_z(0, in_quad[k - 1], zl)
+
+    @pl.when(late == 1)
+    def _():
+        signal(ready_cross, opposite)
+        send_z(1, opposite, zl)
+
+    xbuf[own] = layer_norm(x_raw[0])
+
+
     for k in range(1, X):
 
         @pl.when(cx + k >= X)
@@ -181,24 +206,6 @@
     def _():
         signal(ready_core, sibling)
         send_x(own, 0, sibling)
-
-    for k in range(1, Y):
-
-        @pl.when(y + k >= Y)
-        def _(k=k):
-            signal(ready_y, along_y[k - 1])
-
-    for k in range(1, QUAD):
-
-        @pl.when(place_z + k >= QUAD)
-        def _(k=k):
-            signal(ready_near, in_quad[k - 1])
-            send_z(0, in_quad[k - 1], zl)
-
-    @pl.when(late == 1)
-    def _():
-        signal(ready_cross, opposite)
-        send_z(1, opposite, zl)
 
     @pl.when(cx < X - 1)
     def _():
@@ -260,11 +267,10 @@
         qexp[g] = jnp.where(row_head == col_head, tiled, jnp.zeros_like(tiled))
 
     loaded(weights.at[pl.ds(1, 2)], 5)
-    wvt[...] = jnp.transpose(weights[2])
-
-    def values(h):
-        block = xbuf[pl.ds(h * per_half, per_half)].reshape(half, width)
-        return dot_t(wvt[...], block).astype(BF16)
+
+    def values(first, count):
+        block = xbuf[pl.ds(first, count // rows)].reshape(count, width)
+        return jnp.transpose(dot(block, weights[2]).astype(BF16))
 
     def raw_scores(h, c):
         block = xbuf[pl.ds(block_of(h, 0, c), X)].reshape(quarter, width)
@@ -294,54 +300,65 @@
         send_x(block, 0, sibling)
 
     recv_z(bbuf.at[opposite_z, y], 1)
-    for who in in_quad:
-        send_z(2, who, opposite_z)
+    for k in range(1, QUAD):
+        send_z(1 + QUAD - k, in_quad[k - 1], opposite_z)
+
+    @pl.when(y < Y - 1)
+    def _():
+        pl.semaphore_wait(ready_y, Y - 1 - y)
+
+    hand_on_y(bbuf.at[opposite_z, y])
 
     recv_z(bbuf.at[pl.ds(0, QUAD - 1), y], 0)
 
-    @pl.when(y < Y - 1)
-    def _():
-        pl.semaphore_wait(ready_y, Y - 1 - y)
-
-    hand_on_y(0)
-
-    @pl.when(zh == 0)
+    hand_on_y(bbuf.at[pl.ds(quad * QUAD, QUAD), y])
+
+    @pl.when((zh == 0) & (zl > 0))
     def _():
         pl.semaphore_wait(ready_far, 1)
         send_far()
 
     recv_x(xbuf.at[pl.ds(0, X)], 0)
-    vbuf[:, 0:half] = values(zh)
+    vbuf[:, 0:half] = values(zh * per_half, half)
     for c in range(CORES):
         ebuf[c * quarter : (c + 1) * quarter] = raw_scores(zh, c)
 
     far_block = block_of(1 - zh, cx, core)
 
     def cross_step():
-        recv_z(bbuf.at[pl.ds(0, QUAD - 1), y], 2)
-        hand_on_y(1)
+        for k in range(1, QUAD):
+            there = (1 - quad) * QUAD + (place_z + k) % QUAD
+            recv_z(bbuf.at[there, y], 1 + k)
+            hand_on_y(bbuf.at[there, y])
 
     def far_step():
-        recv_x(far_raw, FAR)
-        xbuf[far_block] = layer_norm(far_raw[0])
-        for k in (2, 1, 3):
-            send_x(far_block, FAR + X - k, along_x[k - 1])
-        send_x(far_block, 2 * X, sibling)
+        for p, piece in enumerate(pieces):
+            recv_x(far_raw.at[0, piece], FAR + X * p)
+            xbuf[far_block, piece] = layer_norm(far_raw[0, piece])
+            for k in (2, 1, 3):
+                send_x(far_block, FAR + X * p + X - k, along_x[k - 1], piece)
+            send_x(far_block, FAR + X * PIECES, sibling, piece)
 
     @pl.when(late == 0)
     def _():
         cross_step()
         far_step()
 
+        @pl.when((zh == 0) & (zl == 0))
+        def _():
+            pl.semaphore_wait(ready_far, 1)
+            send_far()
+
     @pl.when(late == 1)
     def _():
         far_step()
         cross_step()
 
-    for k in (1, 3, 2):
-        block = block_of(1 - zh, other_x(k), core)
-        recv_x(xbuf.at[block], FAR + k)
-        send_x(block, 2 * X, sibling)
+    for p, piece in enumerate(pieces):
+        for k in (1, 3, 2):
+            block = block_of(1 - zh, other_x(k), core)
+            recv_x(xbuf.at[block, piece], FAR + X * p + k)
+            send_x(block, FAR + X * PIECES, sibling, piece)
 
     remote(bbuf.at[pl.ds(0, 2 * (Y - 1))], bys, byr, sibling).wait_recv()
     found = []
@@ -349,9 +366,10 @@
         at = pl.ds(c * quarter, quarter)
         found.append(scores(ebuf[at], at, zh, c))
     found.append(scores(raw_scores(1 - zh, core), part_of(core), 1 - zh, core))
-    recv_x(xbuf.at[pl.ds(0, X)], 2 * X)
+    vbuf[:, part_of(core)] = values(block_of(1 - zh, 0, core), quarter)
+    recv_x(xbuf.at[pl.ds(0, X)], FAR + X * PIECES)
     found.append(scores(raw_scores(1 - zh, 1 - core), part_of(1 - core), 1 - zh, 1 - core))
-    vbuf[:, half:] = values(1 - zh)
+    vbuf[:, part_of(1 - core)] = values(block_of(1 - zh, 0, 1 - core), quarter)
 
     top = functools.reduce(jnp.maximum, [f[1] for f in found])
     shares = [jnp.exp(f[1] - top) for f in found]
@@ -362,13 +380,12 @@
     feature_head = lax.broadcasted_iota(jnp.int32, (group_width, group_lanes), 0) // head_size
     lane_of = lax.broadcasted_iota(jnp.int32, (group_width, group_lanes), 1) // rows
     place = pick[:, :group_lanes].astype(BF16)
-    pieces = []
+    kept = []
     for g in range(2):
         f = slice(g * group_width, (g + 1) * group_width)
         l = slice(g * group_lanes, (g + 1) * group_lanes)
-        kept = jnp.where(feature_head == lane_of, dot(vbuf[f], wbuf[:, l]), 0.0).astype(BF16)
-        pieces.append(dot_t(place, kept).astype(BF16))
-    attended = jnp.concatenate(pieces, axis=1)
+        kept.append(jnp.where(feature_head == lane_of, dot(vbuf[f], wbuf[:, l]), 0.0).astype(BF16))
+    attended = dot_t(place, jnp.concatenate(kept, axis=0)).astype(BF16)
 
     loaded(weights.at[3], 6)
     projected = dot(attended, weights[3])
@@ -414,15 +431,14 @@
             pltpu.VMEM((Z_LO, Y, keys_each, lanes), BF16),
             pltpu.VMEM((width, tokens), BF16),
             pltpu.VMEM((2, lanes // 2, width // 2), BF16),
-            pltpu.VMEM((width, width), BF16),
             pltpu.VMEM((tokens, lanes), F32),
             pltpu.VMEM((tokens, lanes), BF16),
             column, column,
             dma((7,)),
             dma,
-            dma((2 * X + 1,)),
+            dma((3 * X + 1,)),
             dma,
-            dma((3,)),
+            dma((1 + QUAD,)),
             dma,
             dma,
             pltpu.SemaphoreType.REGULAR((6,)),

time: 30.5 us -> 29 us (0.951)
  the two profiles are of different devices: /device:TPU:457 before, /device:TPU:1 now
where the time goes in v4:
time: 29 us; the launch traced here: 28.9 us
  Pallas kernels  27.6 us (95%)
  between operations  0.66 us (2%)
  local copies, waits for them, and re-layouts  0.62 us (2%)
    pallas_call x1, Pallas kernels, shards(): pl.pallas_call(kernel, out_shape=jax.ShapeDtypeStruct((samples, rows, wid...  27.6 us
    unnamed x1, local copies, waits for them, and re-layouts  0.62 us

profile of v4, /device:TPU:1, one launch (start us, length us, event | category | flops | bytes accessed | tf_op | source)
XLA Modules:
  0.0 28.9 jit_solution(2018977875277362663)
XLA Ops:
  0.7 27.6 %shard_map.100 = bf16[1,32,768]{2,1,0:T(8,128)(2,1)S(1)} custom-call(s32[1]{0:T(128)S(6)} %copy.12.step_s, bf16[1,32,768]{2,1,0:T(8,128)(2,1)} %x_hbm.1, bf16[16,16,32]{2,1,0:T(8,128)(2,1)} %bitcast.1, s32[512]{0:T(512)} %chain_hbm.1, s32[512]{0:T(512)} %pad_hbm.1, f32[16]{0:T(128)} %gain_hbm.1, bf16[768,768]{1,0:T(8,128)(2,1)} %wq_hbm.1, ...), custom_call_target="tpu_custom_call" | custom-call | tf_op jit(solution)/shard_map/pallas_call | solution.py:418
  28.3 0.6 %copy.13 = bf16[1,32,768]{2,1,0:T(8,128)(2,1)} copy(bf16[1,32,768]{2,1,0:T(8,128)(2,1)S(1)} %shard_map.100) | data formatting | bytes 98304

commit v5 on v4

--- a/solution.py
+++ b/solution.py
@@ -57,7 +57,7 @@
     y, zl = s % Y, s // Y
     core, cx, zh = t % CORES, (t // CORES) % X, t // (CORES * X)
     quad, place_z = zl // QUAD, zl % QUAD
-    late = (quad + zh * (place_z // 2)) % 2
+    late = quad
     ready_x, ready_core, ready_y, ready_near, ready_cross, ready_far = (ready.at[n] for n in range(6))
 
     def tok_of(h, x, c):
@@ -80,38 +80,6 @@
     def signal(semaphore, who):
         pl.semaphore_signal(semaphore, inc=1, device_id=who, device_id_type=MESH)
 
-    barrier = pltpu.get_barrier_semaphore()
-
-    @pl.when(zh == 0)
-    def _():
-        signal(barrier, far)
-
-    @pl.when(core == CORES - 1)
-    def _():
-        signal(barrier, sibling)
-
-    for k in range(1, X):
-
-        @pl.when(cx + k < X)
-        def _(k=k):
-            signal(barrier, along_x[k - 1])
-
-    for k in range(1, Y):
-
-        @pl.when(y + k < Y)
-        def _(k=k):
-            signal(barrier, along_y[k - 1])
-
-    for k in range(1, QUAD):
-
-        @pl.when(place_z + k < QUAD)
-        def _(k=k):
-            signal(barrier, in_quad[k - 1])
-
-    @pl.when(late == 0)
-    def _():
-        signal(barrier, opposite)
-
     loads = [
         (x_hbm, x_raw, 0), (bias_hbm, bias_raw, 1), (chain_hbm, small.at[0], 2), (pad_hbm, small.at[1], 2),
         (gain_hbm, gain_s, 3), (wq_hbm, weights.at[0], 4), (wk_hbm, weights.at[1], 5), (wv_hbm, weights.at[2], 5),
@@ -119,6 +87,38 @@
     ]
     for src, dst, n in loads:
         pltpu.make_async_copy(src, dst, lsem.at[n]).start()
+
+    barrier = pltpu.get_barrier_semaphore()
+
+    @pl.when(zh == 0)
+    def _():
+        signal(barrier, far)
+
+    @pl.when(core == CORES - 1)
+    def _():
+        signal(barrier, sibling)
+
+    for k in range(1, X):
+
+        @pl.when(cx + k < X)
+        def _(k=k):
+            signal(barrier, along_x[k - 1])
+
+    for k in range(1, Y):
+
+        @pl.when(y + k < Y)
+        def _(k=k):
+            signal(barrier, along_y[k - 1])
+
+    for k in range(1, QUAD):
+
+        @pl.when(place_z + k < QUAD)
+        def _(k=k):
+            signal(barrier, in_quad[k - 1])
+
+    @pl.when(late == 0)
+    def _():
+        signal(barrier, opposite)
 
     def loaded(ref, n):
         pltpu.make_async_copy(ref, ref, lsem.at[n]).wait()
@@ -360,13 +360,14 @@
             recv_x(xbuf.at[block, piece], FAR + X * p + k)
             send_x(block, FAR + X * PIECES, sibling, piece)
 
+    raw = raw_scores(1 - zh, core)
+    vbuf[:, part_of(core)] = values(block_of(1 - zh, 0, core), quarter)
     remote(bbuf.at[pl.ds(0, 2 * (Y - 1))], bys, byr, sibling).wait_recv()
     found = []
     for c in range(CORES):
         at = pl.ds(c * quarter, quarter)
         found.append(scores(ebuf[at], at, zh, c))
-    found.append(scores(raw_scores(1 - zh, core), part_of(core), 1 - zh, core))
-    vbuf[:, part_of(core)] = values(block_of(1 - zh, 0, core), quarter)
+    found.append(scores(raw, part_of(core), 1 - zh, core))
     recv_x(xbuf.at[pl.ds(0, X)], FAR + X * PIECES)
     found.append(scores(raw_scores(1 - zh, 1 - core), part_of(1 - core), 1 - zh, 1 - core))
     vbuf[:, part_of(1 - core)] = values(block_of(1 - zh, 0, 1 - core), quarter)

time: 29 us -> 29 us (level)
  no operation moved by 1% of the time
where the time goes in v5:
time: 29 us; the launch traced here: 28.8 us
  Pallas kernels  27.6 us (95%)
  between operations  0.66 us (2%)
  local copies, waits for them, and re-layouts  0.62 us (2%)
    pallas_call x1, Pallas kernels, shards(): pl.pallas_call(kernel, out_shape=jax.ShapeDtypeStruct((samples, rows, wid...  27.6 us
    unnamed x1, local copies, waits for them, and re-layouts  0.62 us

profile of v5, /device:TPU:1, one launch (start us, length us, event | category | flops | bytes accessed | tf_op | source)
XLA Modules:
  0.0 28.8 jit_solution(8534326145849319717)
XLA Ops:
  0.7 27.6 %shard_map.100 = bf16[1,32,768]{2,1,0:T(8,128)(2,1)S(1)} custom-call(s32[1]{0:T(128)S(6)} %copy.12.step_s, bf16[1,32,768]{2,1,0:T(8,128)(2,1)} %x_hbm.1, bf16[16,16,32]{2,1,0:T(8,128)(2,1)} %bitcast.1, s32[512]{0:T(512)} %chain_hbm.1, s32[512]{0:T(512)} %pad_hbm.1, f32[16]{0:T(128)} %gain_hbm.1, bf16[768,768]{1,0:T(8,128)(2,1)} %wq_hbm.1, ...), custom_call_target="tpu_custom_call" | custom-call | tf_op jit(solution)/shard_map/pallas_call | solution.py:419
  28.2 0.6 %copy.13 = bf16[1,32,768]{2,1,0:T(8,128)(2,1)} copy(bf16[1,32,768]{2,1,0:T(8,128)(2,1)S(1)} %shard_map.100) | data formatting | bytes 98304

commit v6 on v4

--- a/solution.py
+++ b/solution.py
@@ -114,8 +114,8 @@
 
     loads = [
         (x_hbm, x_raw, 0), (bias_hbm, bias_raw, 1), (chain_hbm, small.at[0], 2), (pad_hbm, small.at[1], 2),
-        (gain_hbm, gain_s, 3), (wq_hbm, weights.at[0], 4), (wk_hbm, weights.at[1], 5), (wv_hbm, weights.at[2], 5),
-        (wo_hbm, weights.at[3], 6),
+        (gain_hbm, gain_s, 3), (wq_hbm, weights.at[0], 4), (wk_hbm, weights.at[1], 4), (wv_hbm, weights.at[2], 4),
+        (wo_hbm, weights.at[3], 4),
     ]
     for src, dst, n in loads:
         pltpu.make_async_copy(src, dst, lsem.at[n]).start()
@@ -128,7 +128,7 @@
             src_ref=ref, dst_ref=ref, send_sem=send, recv_sem=recv, device_id=who, device_id_type=MESH
         )
 
-    FAR = X
+    FAR = 2
 
     def send_x(block, n, who, piece=slice(None)):
         remote(xbuf.at[block, piece], xs, xr.at[n], who).start()
@@ -200,7 +200,7 @@
         @pl.when(cx + k >= X)
         def _(k=k):
             signal(ready_x, along_x[k - 1])
-            send_x(own, X - k, along_x[k - 1])
+            send_x(own, 1, along_x[k - 1])
 
     @pl.when(core == 0)
     def _():
@@ -215,7 +215,7 @@
 
         @pl.when(cx + k < X)
         def _(k=k):
-            send_x(own, X - k, along_x[k - 1])
+            send_x(own, 1, along_x[k - 1])
 
     @pl.when(place_z < QUAD - 1)
     def _():
@@ -254,7 +254,7 @@
     for h in range(heads):
         gain = jnp.where(lane_head == h, gain_s[h], gain)
 
-    loaded(weights.at[0], 4)
+    loaded(weights, 4)
     queries = dot(xbuf[own], weights[0]).astype(BF16)
     group_heads = heads // 2
     group_width = width // 2
@@ -266,7 +266,6 @@
         tiled = jnp.concatenate([part] * group_heads, axis=0)
         qexp[g] = jnp.where(row_head == col_head, tiled, jnp.zeros_like(tiled))
 
-    loaded(weights.at[pl.ds(1, 2)], 5)
 
     def values(first, count):
         block = xbuf[pl.ds(first, count // rows)].reshape(count, width)
@@ -294,10 +293,9 @@
     def part_of(c):
         return pl.ds(pl.multiple_of(half + c * quarter, quarter), quarter)
 
+    recv_x(xbuf.at[pl.ds(0, X - 1)], 1)
     for k in range(1, X):
-        block = block_of(zh, other_x(k), core)
-        recv_x(xbuf.at[block], k)
-        send_x(block, 0, sibling)
+        send_x(block_of(zh, other_x(k), core), 0, sibling)
 
     recv_z(bbuf.at[opposite_z, y], 1)
     for k in range(1, QUAD):
@@ -387,7 +385,6 @@
         kept.append(jnp.where(feature_head == lane_of, dot(vbuf[f], wbuf[:, l]), 0.0).astype(BF16))
     attended = dot_t(place, jnp.concatenate(kept, axis=0)).astype(BF16)
 
-    loaded(weights.at[3], 6)
     projected = dot(attended, weights[3])
     ratio = jnp.full((1, width), step_s[0], jnp.int32).astype(F32) / (STEPS - 1)
     upper, lower = SIGMA_TOP ** (1.0 / RHO), SIGMA_LOW ** (1.0 / RHO)
@@ -434,9 +431,9 @@
             pltpu.VMEM((tokens, lanes), F32),
             pltpu.VMEM((tokens, lanes), BF16),
             column, column,
-            dma((7,)),
+            dma((5,)),
             dma,
-            dma((3 * X + 1,)),
+            dma((2 * X + 3,)),
             dma,
             dma((1 + QUAD,)),
             dma,

time: 29 us -> 28.9 us (level)
  no operation moved by 1% of the time
where the time goes in v6:
time: 28.9 us; the launch traced here: 28.8 us
  Pallas kernels  27.5 us (95%)
  between operations  0.66 us (2%)
  local copies, waits for them, and re-layouts  0.62 us (2%)
    pallas_call x1, Pallas kernels, shards(): pl.pallas_call(kernel, out_shape=jax.ShapeDtypeStruct((samples, rows, wid...  27.5 us
    unnamed x1, local copies, waits for them, and re-layouts  0.62 us

profile of v6, /device:TPU:1, one launch (start us, length us, event | category | flops | bytes accessed | tf_op | source)
XLA Modules:
  0.0 28.8 jit_solution(6561827197195295279)
XLA Ops:
  0.7 27.5 %shard_map.100 = bf16[1,32,768]{2,1,0:T(8,128)(2,1)S(1)} custom-call(s32[1]{0:T(128)S(6)} %copy.12.step_s, bf16[1,32,768]{2,1,0:T(8,128)(2,1)} %x_hbm.1, bf16[16,16,32]{2,1,0:T(8,128)(2,1)} %bitcast.1, s32[512]{0:T(512)} %chain_hbm.1, s32[512]{0:T(512)} %pad_hbm.1, f32[16]{0:T(128)} %gain_hbm.1, bf16[768,768]{1,0:T(8,128)(2,1)} %wq_hbm.1, ...), custom_call_target="tpu_custom_call" | custom-call | tf_op jit(solution)/shard_map/pallas_call | solution.py:415
  28.1 0.6 %copy.13 = bf16[1,32,768]{2,1,0:T(8,128)(2,1)} copy(bf16[1,32,768]{2,1,0:T(8,128)(2,1)S(1)} %shard_map.100) | data formatting | bytes 98304
